TPU v7x, 32 devices: a whole 2x2x4 slice. The times are simulated.
32 devices in a mesh: grp: 2 (over x), cell: 16 (over z, y, core).
Axes of the slice: x: 2, y: 2, z: 4, core: 2. Of those that a mesh axis runs over, the one named last changes fastest.
Arguments:
- fields: bfloat16 [8192, 3, 8192], P(('grp', 'cell')), parts along dimension 0, may hold values from -6 to 6
- horiz: float32 [16384], P(('grp', 'cell')), parts along dimension 0, may hold values from 0.2 to 1
- vertical: float32 [16384], P(('grp', 'cell')), parts along dimension 0, may hold values from 1.5 to 6
- tilt_angle: float32 [16384], P(('grp', 'cell')), parts along dimension 0, may hold values from 0.2 to 1.4
- azimuth: float32 [16384], P(('grp', 'cell')), parts along dimension 0, may hold values from -3.140625 to 3.140625
- electrode_quads: int32 [4096, 4], P('grp'), parts along dimension 0, may hold values from 0 to 4095, as said below
Outputs:
- jacobian: bfloat16 [4096, 4, 8192], P('grp', None, 'cell'), parts along dimension 0
- coverage: float32 [16384], P(('grp', 'cell')), parts along dimension 0
There are 2 independent parts, one for each index of `grp`. A program takes and returns all parts, laid end to end along the dimension named above; each array names one. Nothing has to cross between parts.
Inputs may be any that keep to these rules, and one draw needn't show every extreme that they name: `electrode_quads`: each row names four different electrodes.
All inputs are finite; a program needn't handle non-finite values.
Results may differ from a plain program's by a relative error of at most 0.001.
Values may be sent and summed in bfloat16 or wider, within the bound.
A program may use at most 192 MiB of HBM per device.

v0:
```python
import jax
import jax.numpy as jnp
from jax import lax
from jax.sharding import PartitionSpec as P


def sensitivity(grads, horiz, vertical, tilt_angle, azimuth, rows):

    def pick(column):
        return jnp.take(grads, rows[:, column], axis=0).astype(jnp.float32)

    source = pick(0) - pick(1)
    receiver = pick(2) - pick(3)
    sin_t = jnp.sin(tilt_angle)
    cos_t = jnp.cos(tilt_angle)
    sin_p = jnp.sin(azimuth)
    cos_p = jnp.cos(azimuth)
    axis_dir = jnp.stack([sin_t * cos_p, sin_t * sin_p, cos_t])
    tilt_dir = jnp.stack([cos_t * cos_p, cos_t * sin_p, -sin_t])
    turn_dir = jnp.stack([-sin_t * sin_p, sin_t * cos_p, jnp.zeros_like(sin_t)])

    def along(field, direction):
        return jnp.sum(field * direction[None], axis=1)

    s_axis = along(source, axis_dir)
    r_axis = along(receiver, axis_dir)
    s_tilt = along(source, tilt_dir)
    r_tilt = along(receiver, tilt_dir)
    s_turn = along(source, turn_dir)
    r_turn = along(receiver, turn_dir)
    inner = jnp.sum(source * receiver, axis=1)
    contrast = vertical - horiz
    return jnp.stack(
        [
            -horiz * (inner - s_axis * r_axis),
            -vertical * s_axis * r_axis,
            -contrast * (s_tilt * r_axis + s_axis * r_tilt),
            -contrast * (s_turn * r_axis + s_axis * r_turn),
        ],
        axis=1,
    )


def local(fields, horiz, vertical, tilt_angle, azimuth, electrode_quads):
    shards = lax.axis_size("cell")
    cell_dev = horiz.shape[0]
    local_fields = lax.all_to_all(fields, "cell", split_axis=2, concat_axis=0, tiled=True)
    values = sensitivity(local_fields, horiz, vertical, tilt_angle, azimuth, electrode_quads)
    partial_sq = jnp.sum(values * values, axis=(1, 2))
    total_sq = lax.psum(partial_sq, "cell")
    meansq = total_sq / (4.0 * cell_dev * shards)
    normed = values * lax.rsqrt(meansq + 1e-06)[:, None, None]
    return (normed.astype(jnp.bfloat16), jnp.sum(normed * normed, axis=(0, 1)))


def solution(mesh):
    placed = (
        P(("grp", "cell"), None, None),
        P(("grp", "cell")),
        P(("grp", "cell")),
        P(("grp", "cell")),
        P(("grp", "cell")),
        P("grp", None),
    )
    return jax.shard_map(
        local,
        mesh=mesh,
        in_specs=placed,
        out_specs=(P("grp", None, "cell"), P(("grp", "cell"))),
        check_vma=False,
    )
```

profile of v0, /device:TPU:0, one launch (start us, length us, event | category | flops | bytes accessed | tf_op | source)
XLA Modules:
  0.0 745.1 jit_solution(583494292606352755)
XLA Ops:
  0.6 25.0 %copy.16 = bf16[256,3,8192]{0,1,2:T(4,128)(2,1)} copy(bf16[256,3,8192]{2,0,1:T(8,128)(2,1)} %param.8) | data formatting | bytes 25165824 | tf_op args[0]
  25.6 0.0 copy-start.5
  25.6 0.0 copy-start.6
  25.6 0.0 copy-start.3
  25.6 0.0 copy-start.4
  25.6 0.0 copy-start.2
  25.6 7.6 %all-to-all-start = ((bf16[256,3,8192]{0,1,2:T(4,128)(2,1)}), bf16[256,3,8192]{0,1,2:T(4,128)(2,1)}, u32[]{:S(2)}, u32[]{:S(2)}) async-start(bf16[256,3,8192]{0,1,2:T(4,128)(2,1)} %copy.16), calls=%async_computation | async-start | bytes 33554432 | tf_op jit(solution)/shard_map/all_to_all | solution.py:47
  33.2 0.1 pad.6.clone
  33.3 0.0 copy-done.5
  33.3 0.0 copy-done.6
  33.4 0.0 copy-done.3
  33.4 0.0 copy-done.4
  33.4 0.0 copy-done.2
  33.5 0.1 pad_maximum_fusion.1
  33.6 296.4 %all-to-all-done = bf16[256,3,8192]{0,1,2:T(4,128)(2,1)} async-done(((bf16[256,3,8192]{0,1,2:T(4,128)(2,1)}), bf16[256,3,8192]{0,1,2:T(4,128)(2,1)}, u32[]{:S(2)}, u32[]{:S(2)}) %all-to-all-start) | async-done | bytes 12582944 | tf_op jit(solution)/shard_map/all_to_all | solution.py:47
  330.0 13.2 %copy.17 = bf16[256,3,8192]{0,2,1:T(8,128)(2,1)} copy(bf16[256,3,8192]{0,1,2:T(4,128)(2,1)} %all-to-all-done) | data formatting | bytes 25165824 | tf_op jit(solution)/shard_map/all_to_all | solution.py:47
  343.1 16.6 %copy.18 = bf16[16,256,3,512]{3,1,0,2:T(8,128)(2,1)} copy(bf16[16,256,3,512]{1,3,0,2:T(8,128)(2,1)} %bitcast.54) | data formatting | bytes 25165824 | tf_op jit(solution)/shard_map/all_to_all | solution.py:47
  359.7 18.9 %copy.19 = bf16[4096,3,512]{2,1,0:T(4,128)(2,1)} copy(bf16[4096,3,512]{2,0,1:T(8,128)(2,1)} %bitcast.55) | data formatting | bytes 25165824 | tf_op jit(solution)/shard_map/all_to_all | solution.py:47
  378.6 26.7 %gather_fusion = bf16[2048,3,512]{2,1,0:T(4,128)(2,1)} fusion(bf16[4096,3,512]{2,1,0:T(4,128)(2,1)} %copy.19, s32[2048]{0:T(1024)S(1)} %fusion.6), kind=kCustom, calls=%fused_computation.clone | custom fusion | bytes 12591104 | tf_op jit(solution)/shard_map/jit(_take)/gather | solution.py:10
  405.2 26.9 %gather_fusion.1 = bf16[2048,3,512]{2,1,0:T(4,128)(2,1)} fusion(bf16[4096,3,512]{2,1,0:T(4,128)(2,1)} %copy.19, s32[2048]{0:T(1024)S(1)} %fusion.7), kind=kCustom, calls=%fused_computation.1.clone | custom fusion | bytes 12591104 | tf_op jit(solution)/shard_map/jit(_take)/gather | solution.py:10
  432.1 27.0 %gather_fusion.2 = bf16[2048,3,512]{2,1,0:T(4,128)(2,1)} fusion(bf16[4096,3,512]{2,1,0:T(4,128)(2,1)} %copy.19, s32[2048]{0:T(1024)S(1)} %fusion.8), kind=kCustom, calls=%fused_computation.2.clone | custom fusion | bytes 12591104 | tf_op jit(solution)/shard_map/jit(_take)/gather | solution.py:10
  459.1 26.8 %gather_fusion.3 = bf16[2048,3,512]{2,1,0:T(4,128)(2,1)} fusion(bf16[4096,3,512]{2,1,0:T(4,128)(2,1)} %copy.19, s32[2048]{0:T(1024)S(1)} %fusion.9), kind=kCustom, calls=%fused_computation.3.clone | custom fusion | bytes 12591104 | tf_op jit(solution)/shard_map/jit(_take)/gather | solution.py:10
  485.9 103.7 %multiply_reduce_fusion.8 = (f32[2048,512]{1,0:T(8,128)}, f32[2048,512]{1,0:T(8,128)}, f32[2048,512]{1,0:T(8,128)}, f32[2048,512]{1,0:T(8,128)}, f32[2048,512]{1...) fusion(bf16[2048,3,512]{2,1,0:T(4,128)(2,1)} %gather_fusion, pred[2048]{0:T(1024)(128)(4,1)S(1)} %get-tuple-element.48, ...), kind=kLoop, calls=%fused_computation.13 | loop fusion | flops 68157440 | bytes 54552576 | tf_op jit(solution)/shard_map/reduce_sum | solution.py:31
  589.6 14.0 %fusion.5 = (f32[2048,1,512]{2,0,1:T(8,128)S(1)}, f32[2048,1,512]{2,0,1:T(8,128)S(1)}, f32[2048,1,512]{2,0,1:T(8,128)}, f32[2048,1,512]{2,0,1:T(8,128)}) fusion(f32[2048,512]{1,0:T(8,128)} %get-tuple-element.14, f32[2048,512]{1,0:T(8,128)} %get-tuple-element.15, f32[2048,512]{1,0:T(8,128)} %get-tuple-element.9, f32[512]{0:T(512)S(1)} %get-tuple-element.34, ...), kind=kLoop, calls=%fused_computation.32 | loop fusion | flops 13631488 | bytes 46143488 | tf_op jit(solution)/shard_map/mul | solution.py:35
  603.6 0.0 copy-start
  603.6 0.0 copy-start.1
  603.6 2.0 copy-done
  605.6 1.2 copy-done.1
  606.8 4.6 multiply_reduce_fusion.1
  611.4 98.9 %psum.7 = f32[2048]{0:T(1024)S(1)} all-reduce(f32[2048]{0:T(1024)S(1)} %multiply_reduce_fusion.1), channel_id=1, replica_groups=mesh['grp'=2,'cell'=16] {'cell'}, use_global_device_ids=true, to_apply=%region_8.10 | all-reduce | flops 2048 | bytes 16384 | tf_op jit(solution)/shard_map/psum | solution.py:50
  710.3 7.5 %multiply_reduce_fusion = (f32[512]{0:T(512)}, bf16[2048,4,512]{2,0,1:T(8,128)(2,1)S(1)}) fusion(f32[2048]{0:T(1024)S(1)} %add_rsqrt_fusion, f32[2048,1,512]{2,0,1:T(8,128)} %get-tuple-element.22, f32[2048,1,512]{2,0,1:T(8,128)} %get-tuple-element.23, f32[2048,1,512]{2,0,1:T(8,128)} %copy-done.1, f32[2048,1,512]{2,0,1:T(8,128)} %copy-done), kind=kLoop, calls=%fused_computation.5 | loop fusion | flops 29359616 | bytes 25176064 | tf_op jit(solution)/shard_map/reduce_sum | solution.py:53
  717.8 27.3 %copy.23 = bf16[2048,4,512]{2,1,0:T(4,128)(2,1)} copy(bf16[2048,4,512]{2,0,1:T(8,128)(2,1)S(1)} %get-tuple-element.17) | data formatting | bytes 16777216
  (12 shorter events, 0.2 us)
Async XLA Ops:
  25.6 7.7 %copy-start.5 = (f32[512]{0:T(512)S(1)}, f32[512]{0:T(512)}, u32[]{:S(2)}) copy-start(f32[512]{0:T(512)} %param.11) | copy-start | bytes 6148
  25.6 7.7 %copy-start.6 = (f32[512]{0:T(512)S(1)}, f32[512]{0:T(512)}, u32[]{:S(2)}) copy-start(f32[512]{0:T(512)} %param.12) | copy-start | bytes 6148
  25.6 7.8 %copy-start.3 = (f32[512]{0:T(512)S(1)}, f32[512]{0:T(512)}, u32[]{:S(2)}) copy-start(f32[512]{0:T(512)} %param.9) | copy-start | bytes 6148
  25.6 7.8 %copy-start.4 = (f32[512]{0:T(512)S(1)}, f32[512]{0:T(512)}, u32[]{:S(2)}) copy-start(f32[512]{0:T(512)} %param.10) | copy-start | bytes 6148
  25.6 7.8 %copy-start.2 = (s32[2048,4]{0,1:T(4,128)S(1)}, s32[2048,4]{0,1:T(4,128)}, u32[]{:S(2)}) copy-start(s32[2048,4]{0,1:T(4,128)} %param.13) | copy-start | bytes 98308
  25.6 304.4 %all-to-all-start = ((bf16[256,3,8192]{0,1,2:T(4,128)(2,1)}), bf16[256,3,8192]{0,1,2:T(4,128)(2,1)}, u32[]{:S(2)}, u32[]{:S(2)}) async-start(bf16[256,3,8192]{0,1,2:T(4,128)(2,1)} %copy.16), calls=%async_computation | async-start | bytes 33554432 | tf_op jit(solution)/shard_map/all_to_all | solution.py:47
  603.6 2.0 copy-start
  603.6 3.2 copy-start.1
where the time goes:
time: 747 us; the launch traced here: 745 us
  waiting for transfers between devices  296 us (40%)
  local copies, waits for them, and re-layouts  212 us (28%)
  other arithmetic  130 us (17%)
  blocking collectives  98.9 us (13%)
  starting transfers between devices  7.58 us (1%)
    all_to_all x1, waiting for transfers between devices, local(): lax.all_to_all(fields, 'cell', split_axis=2, concat_axis=0, tiled=True)  296 us
    gather x4, local copies, waits for them, and re-layouts, pick(): return jnp.take(grads, rows[:, column], axis=0).astype(jnp.float32)  107 us
    reduce_sum x1, other arithmetic, sensitivity(): inner = jnp.sum(source * receiver, axis=1)  104 us
    psum x1, blocking collectives, local(): total_sq = lax.psum(partial_sq, 'cell')  98.9 us
    unnamed x16, local copies, waits for them, and re-layouts  55.5 us
    all_to_all x3, local copies, waits for them, and re-layouts, local(): lax.all_to_all(fields, 'cell', split_axis=2, concat_axis=0, tiled=True)  48.6 us
  transfers between devices with their start and end apart: 1, of which 1 were waited for; matrix products, arithmetic and copies ran while one was open for 0% of the time, Pallas kernels for 0%

commit v1 on v0

v1 whole, which is shorter than its diff:
```python
import functools

import jax
import jax.numpy as jnp
from jax import lax
from jax.experimental import pallas as pl
from jax.experimental.pallas import tpu as pltpu
from jax.sharding import PartitionSpec as P

MESH = pl.DeviceIdType.MESH
LANES = 128


def greet(n, me):
    barrier = pltpu.get_barrier_semaphore()

    @pl.loop(1, n)
    def _(step):
        pl.semaphore_signal(barrier, inc=1, device_id={"cell": lax.rem(me + step, n)}, device_id_type=MESH)

    pl.semaphore_wait(barrier, n - 1)


def exchange_kernel(n, fields, gathered, send_sem, recv_sem, own_sem):
    me = lax.axis_index("cell")
    rows = fields.shape[1]
    cells = gathered.shape[2]
    greet(n, me)

    def landing(step):
        return gathered.at[:, pl.ds(pl.multiple_of(me * rows, rows), rows), :]

    def leaving(device):
        return fields.at[:, :, pl.ds(pl.multiple_of(device * cells, cells), cells)]

    def copy(step):
        peer = lax.rem(me + step, n)
        return pltpu.make_async_remote_copy(
            src_ref=leaving(peer),
            dst_ref=landing(step),
            send_sem=send_sem.at[step],
            recv_sem=recv_sem.at[step],
            device_id={"cell": peer},
            device_id_type=MESH,
        )

    @pl.loop(1, n)
    def _(step):
        copy(step).start()

    own = pltpu.make_async_copy(leaving(me), landing(0), own_sem)
    own.start()
    own.wait()

    @pl.loop(1, n)
    def _(step):
        copy(step).wait()


def exchange(fields, n, cells):
    comps, rows, _ = fields.shape
    return pl.pallas_call(
        functools.partial(exchange_kernel, n),
        out_shape=jax.ShapeDtypeStruct((comps, rows * n, cells), fields.dtype),
        in_specs=[pl.BlockSpec(memory_space=pl.ANY)],
        out_specs=pl.BlockSpec(memory_space=pl.ANY),
        scratch_shapes=[
            pltpu.SemaphoreType.DMA((n,)),
            pltpu.SemaphoreType.DMA((n,)),
            pltpu.SemaphoreType.DMA,
        ],
        compiler_params=pltpu.CompilerParams(collective_id=0, has_side_effects=True),
        name="exchange",
    )(fields)


def total_kernel(n, part, total, slots, send_sem, recv_sem):
    me = lax.axis_index("cell")
    greet(n, me)

    def copy(step):
        return pltpu.make_async_remote_copy(
            src_ref=part,
            dst_ref=slots.at[step],
            send_sem=send_sem.at[step],
            recv_sem=recv_sem.at[step],
            device_id={"cell": lax.rem(me + step, n)},
            device_id_type=MESH,
        )

    @pl.loop(1, n)
    def _(step):
        copy(step).start()

    slots[0] = part[...]

    @pl.loop(1, n)
    def _(step):
        copy(step).wait()

    total[...] = jnp.sum(slots[...], axis=0)


def total_of(part, n):
    return pl.pallas_call(
        functools.partial(total_kernel, n),
        out_shape=jax.ShapeDtypeStruct(part.shape, part.dtype),
        in_specs=[pl.BlockSpec(memory_space=pltpu.VMEM)],
        out_specs=pl.BlockSpec(memory_space=pltpu.VMEM),
        scratch_shapes=[
            pltpu.VMEM((n, *part.shape), part.dtype),
            pltpu.SemaphoreType.DMA((n,)),
            pltpu.SemaphoreType.DMA((n,)),
        ],
        compiler_params=pltpu.CompilerParams(collective_id=1, has_side_effects=True),
        name="total",
    )(part)


def sens_kernel(quads, grads, coef, sens, squares, wide, diffs):
    comps, electrodes, _ = grads.shape
    readings = squares.shape[0]
    chunk = pl.program_id(0)
    block = 256

    for c in range(comps):

        @pl.loop(0, electrodes // block)
        def _(i):
            at = pl.multiple_of(i * block, block)
            wide[pl.ds(c * electrodes + at, block), :] = grads[c, pl.ds(at, block), :].astype(jnp.float32)

    @pl.loop(0, readings // 8)
    def _(g):
        for u in range(8):
            q = g * 8 + u
            a, b, m, n = (quads[4 * q + j] for j in range(4))
            for c in range(comps):
                base = c * electrodes
                diffs[c, pl.ds(q, 1), :] = wide[pl.ds(base + a, 1), :] - wide[pl.ds(base + b, 1), :]
                diffs[comps + c, pl.ds(q, 1), :] = wide[pl.ds(base + m, 1), :] - wide[pl.ds(base + n, 1), :]

    tile = 16

    @pl.loop(0, readings // tile)
    def _(i):
        at = pl.multiple_of(i * tile, tile)
        s = [diffs[c, pl.ds(at, tile), :] for c in range(3)]
        r = [diffs[3 + c, pl.ds(at, tile), :] for c in range(3)]
        terms = [s[c] * r[c] for c in range(3)]
        terms += [s[i] * r[j] + s[j] * r[i] for i, j in ((0, 1), (0, 2), (1, 2))]
        square = None
        for p in range(4):
            value = terms[0] * coef[pl.ds(6 * p, 1), :]
            for k in range(1, 6):
                value = value + terms[k] * coef[pl.ds(6 * p + k, 1), :]
            sens[pl.ds(4 * at + p, tile, stride=4), :] = value
            square = value * value if square is None else square + value * value

        @pl.when(chunk == 0)
        def _():
            squares[pl.ds(at, tile), :] = square

        @pl.when(chunk > 0)
        def _():
            squares[pl.ds(at, tile), :] += square


def sensitivities(quads, gathered, coef):
    comps, electrodes, cells = gathered.shape
    readings = quads.shape[0] // 4
    return pl.pallas_call(
        sens_kernel,
        grid_spec=pltpu.PrefetchScalarGridSpec(
            num_scalar_prefetch=1,
            grid=(cells // LANES,),
            in_specs=[
                pl.BlockSpec((comps, electrodes, LANES), lambda k, _: (0, 0, k)),
                pl.BlockSpec((coef.shape[0], LANES), lambda k, _: (0, k)),
            ],
            out_specs=[
                pl.BlockSpec((readings * 4, LANES), lambda k, _: (0, k)),
                pl.BlockSpec((readings, LANES), lambda k, _: (0, 0)),
            ],
            scratch_shapes=[
                pltpu.VMEM((comps * electrodes, LANES), jnp.float32),
                pltpu.VMEM((2 * comps, readings, LANES), jnp.float32),
            ],
        ),
        out_shape=[
            jax.ShapeDtypeStruct((readings * 4, cells), jnp.float32),
            jax.ShapeDtypeStruct((readings, LANES), jnp.float32),
        ],
        compiler_params=pltpu.CompilerParams(vmem_limit_bytes=56 * 2**20),
        name="sens",
    )(quads, gathered, coef)


def norm_kernel(sens, scale, jacobian, coverage):
    count = sens.shape[0]

    @pl.when(pl.program_id(0) == 0)
    def _():
        coverage[...] = jnp.zeros_like(coverage)

    for lane in range(sens.shape[1] // LANES):
        at = pl.ds(lane * LANES, LANES)
        normed = sens[:, at] * scale[...]
        jacobian[:, :, at] = normed.reshape(count // 4, 4, LANES).astype(jnp.bfloat16)
        coverage[:, at] += jnp.sum((normed * normed).reshape(count // 8, 8, LANES), axis=0)


def normalise(sens, scale):
    rows, cells = sens.shape
    block = 1024
    return pl.pallas_call(
        norm_kernel,
        grid=(rows // block,),
        in_specs=[
            pl.BlockSpec((block, cells), lambda i: (i, 0)),
            pl.BlockSpec((block, LANES), lambda i: (i, 0)),
        ],
        out_specs=[
            pl.BlockSpec((block // 4, 4, cells), lambda i: (i, 0, 0)),
            pl.BlockSpec((8, cells), lambda i: (0, 0)),
        ],
        out_shape=[
            jax.ShapeDtypeStruct((rows // 4, 4, cells), jnp.bfloat16),
            jax.ShapeDtypeStruct((8, cells), jnp.float32),
        ],
        compiler_params=pltpu.CompilerParams(vmem_limit_bytes=48 * 2**20),
        name="norm",
    )(sens, scale)


def coefficients(horiz, vertical, tilt_angle, azimuth):
    sin_t, cos_t = jnp.sin(tilt_angle), jnp.cos(tilt_angle)
    sin_p, cos_p = jnp.sin(azimuth), jnp.cos(azimuth)
    axis = (sin_t * cos_p, sin_t * sin_p, cos_t)
    tilt = (cos_t * cos_p, cos_t * sin_p, -sin_t)
    turn = (-sin_t * sin_p, sin_t * cos_p, jnp.zeros_like(sin_t))
    contrast = vertical - horiz
    pairs = ((0, 0), (1, 1), (2, 2), (0, 1), (0, 2), (1, 2))
    rows = [-horiz * ((1.0 if i == j else 0.0) - axis[i] * axis[j]) for i, j in pairs]
    rows += [-vertical * axis[i] * axis[j] for i, j in pairs]
    for other in (tilt, turn):
        rows += [-contrast * (other[i] * axis[j] + axis[i] * other[j]) for i, j in pairs]
    return jnp.stack(rows)


def local(fields, horiz, vertical, tilt_angle, azimuth, electrode_quads):
    shards = lax.axis_size("cell")
    cells = horiz.shape[0]
    readings = electrode_quads.shape[0]
    gathered = exchange(fields.transpose(1, 0, 2), shards, cells)
    coef = coefficients(horiz, vertical, tilt_angle, azimuth)
    sens, squares = sensitivities(electrode_quads.reshape(-1), gathered, coef)
    part = jnp.sum(squares, axis=1).reshape(readings // LANES, LANES)
    meansq = total_of(part, shards).reshape(-1) / (4.0 * cells * shards)
    scale = jnp.broadcast_to(lax.rsqrt(meansq + 1e-06)[:, None, None], (readings, 4, LANES))
    jacobian, coverage = normalise(sens, scale.reshape(readings * 4, LANES))
    return jacobian, jnp.sum(coverage, axis=0)


def solution(mesh):
    placed = (
        P(("grp", "cell"), None, None),
        P(("grp", "cell")),
        P(("grp", "cell")),
        P(("grp", "cell")),
        P(("grp", "cell")),
        P("grp", None),
    )
    return jax.shard_map(
        local,
        mesh=mesh,
        in_specs=placed,
        out_specs=(P("grp", None, "cell"), P(("grp", "cell"))),
        check_vma=False,
    )
```

time: 747 us -> 396 us (0.53)
  Pallas kernels: 0 us -> 382 us
  waiting for transfers between devices: 296 us -> 0 us
  local copies, waits for them, and re-layouts: 212 us -> 7.12 us
  other arithmetic: 130 us -> 4.88 us
  blocking collectives: 98.9 us -> 0 us
  starting transfers between devices: 7.58 us -> 0 us
    pallas_call x0 -> x4, Pallas kernels: none -> 382 us  [the longest x1 209 us: exchange(): pl.pallas_call(functools.partial(exchange_kernel, n), out_shape=jax.Shape...]
    all_to_all x1 -> x0, waiting for transfers between devices: 296 us -> none  [local(): lax.all_to_all(fields, 'cell', split_axis=2, concat_axis=0, tiled=True)]
    reduce_sum x3 -> x2, other arithmetic: 116 us -> 2.75 us  [the longest x1 2.16 us: local(): part = jnp.sum(squares, axis=1).reshape(readings // LANES, LANES)]
    gather x4 -> x0, local copies, waits for them, and re-layouts: 107 us -> none  [pick(): return jnp.take(grads, rows[:, column], axis=0).astype(jnp.float32)]
    psum x1 -> x0, blocking collectives: 98.9 us -> none  [local(): total_sq = lax.psum(partial_sq, 'cell')]
    unnamed x16 -> x1, local copies, waits for them, and re-layouts: 55.5 us -> 1.11 us
    all_to_all x3 -> x0, local copies, waits for them, and re-layouts: 48.6 us -> none  [local(): lax.all_to_all(fields, 'cell', split_axis=2, concat_axis=0, tiled=True)]
    mul x2, other arithmetic: 14 us -> 1.42 us  [coefficients(): -contrast * (other[i] * axis[j] + axis[i] * other[j])]
  transfers between devices with their start and end apart: 1 -> 0, of which waited for: 1 -> 0; matrix products, arithmetic and copies ran while one was open for 0% -> 0% of each run, Pallas kernels for 0% -> 0%
where the time goes in v1:
time: 396 us; the launch traced here: 395 us
  Pallas kernels  382 us (96%)
  local copies, waits for them, and re-layouts  7.12 us (2%)
  other arithmetic  4.88 us (1%)
    pallas_call x1, Pallas kernels, exchange(): pl.pallas_call(functools.partial(exchange_kernel, n), out_shape=jax.Shape...  209 us
    pallas_call x1, Pallas kernels, sensitivities(): pl.pallas_call(sens_kernel, grid_spec=pltpu.PrefetchScalarGridSpec(num_sc...  85.1 us
    pallas_call x1, Pallas kernels, total_of(): pl.pallas_call(functools.partial(total_kernel, n), out_shape=jax.ShapeDty...  75.8 us
    pallas_call x1, Pallas kernels, normalise(): pl.pallas_call(norm_kernel, grid=(rows // block,), in_specs=[pl.BlockSpec...  12.2 us

profile of v1, /device:TPU:0, one launch (start us, length us, event | category | flops | bytes accessed | tf_op | source)
XLA Modules:
  0.0 395.2 jit_solution(15299308519644078901)
XLA Ops:
  0.6 0.7 fusion.3
  1.4 0.7 add_multiply_fusion
  2.1 0.7 add_multiply_fusion.1
  2.8 1.9 stack.99.coef
  4.7 1.1 copy.8
  5.8 1.3 reshape.25.quads
  7.1 209.4 %exchange.1.grads = bf16[3,4096,512]{2,1,0:T(8,128)(2,1)} custom-call(bf16[3,256,8192]{2,1,0:T(8,128)(2,1)} %bitcast.28), custom_call_target="tpu_custom_call" | custom-call | tf_op jit(solution)/shard_map/exchange/pallas_call | solution.py:62
  216.5 85.1 %sens.1 = (f32[8192,512]{1,0:T(8,128)}, f32[2048,128]{1,0:T(8,128)}) custom-call(s32[8192]{0:T(1024)} %reshape.25.quads, bf16[3,4096,512]{2,1,0:T(8,128)(2,1)} %exchange.1.grads, f32[24,512]{1,0:T(8,128)} %stack.99.coef), custom_call_target="tpu_custom_call" | custom-call | tf_op jit(solution)/shard_map/sens/pallas_call | solution.py:172
  301.6 2.2 reduce_sum.18
  303.8 75.8 %total.1 = f32[16,128]{1,0:T(8,128)} custom-call(f32[16,128]{1,0:T(8,128)} %bitcast.29), custom_call_target="tpu_custom_call" | custom-call | tf_op jit(solution)/shard_map/total/pallas_call | solution.py:105
  379.6 0.7 rsqrt_bitcast_fusion
  380.3 0.3 broadcast_in_dim.10
  380.6 0.6 broadcast_in_dim.11
  381.3 1.1 broadcast_in_dim.12.scale
  382.4 12.2 %norm.1 = (bf16[2048,4,512]{2,1,0:T(4,128)(2,1)}, f32[8,512]{1,0:T(8,128)S(1)}) custom-call(f32[8192,512]{1,0:T(8,128)} %get-tuple-element.6.sens, f32[8192,128]{1,0:T(8,128)S(1)} %broadcast_in_dim.12.scale), custom_call_target="tpu_custom_call" | custom-call | tf_op jit(solution)/shard_map/norm/pallas_call | solution.py:216
  394.6 0.6 reduce_sum.19

commit v2 on v1

v2 whole, which is shorter than its diff:
```python
import functools

import jax
import jax.numpy as jnp
from jax import lax
from jax.experimental import pallas as pl
from jax.experimental.pallas import tpu as pltpu
from jax.sharding import PartitionSpec as P

MESH = pl.DeviceIdType.MESH
LANES = 128


def greet(n, me):
    barrier = pltpu.get_barrier_semaphore()

    @pl.loop(1, n)
    def _(step):
        pl.semaphore_signal(barrier, inc=1, device_id={"cell": lax.rem(me + step, n)}, device_id_type=MESH)

    pl.semaphore_wait(barrier, n - 1)


def chunk_sensitivities(quads, grads, coef, sens, squares, wide, diffs):
    comps, electrodes, _ = wide.shape
    readings = squares.shape[0]
    block = 256

    @pl.loop(0, electrodes // block)
    def _(i):
        at = pl.multiple_of(i * block, block)
        for c in range(comps):
            wide[c, pl.ds(at, block), :] = grads[c, pl.ds(at, block), :].astype(jnp.float32)

    @pl.loop(0, readings // 8)
    def _(g):
        for u in range(8):
            q = g * 8 + u
            a, b, m, n = (quads[4 * q + j] for j in range(4))
            for c in range(comps):
                diffs[c, pl.ds(q, 1), :] = wide[c, pl.ds(a, 1), :] - wide[c, pl.ds(b, 1), :]
                diffs[comps + c, pl.ds(q, 1), :] = wide[c, pl.ds(m, 1), :] - wide[c, pl.ds(n, 1), :]

    tile = 16

    @pl.loop(0, readings // tile)
    def _(i):
        at = pl.multiple_of(i * tile, tile)
        s = [diffs[c, pl.ds(at, tile), :] for c in range(3)]
        r = [diffs[3 + c, pl.ds(at, tile), :] for c in range(3)]
        terms = [s[c] * r[c] for c in range(3)]
        terms += [s[i] * r[j] + s[j] * r[i] for i, j in ((0, 1), (0, 2), (1, 2))]
        square = squares[pl.ds(at, tile), :]
        for p in range(4):
            value = terms[0] * coef[pl.ds(6 * p, 1), :]
            for k in range(1, 6):
                value = value + terms[k] * coef[pl.ds(6 * p + k, 1), :]
            sens[pl.ds(4 * at + p, tile, stride=4), :] = value
            square = square + value * value
        squares[pl.ds(at, tile), :] = square


def exchange_kernel(
    n, quads, fields, coef, sens, squares, landed, ready, wide, diffs, send_sem, recv_sem, own_sem, out_sem
):
    me = lax.axis_index("cell")
    rows = fields.shape[1]
    chunks = landed.shape[0]
    cells = chunks * LANES
    greet(n, me)

    def landing(chunk):
        return landed.at[chunk, :, pl.ds(pl.multiple_of(me * rows, rows), rows), :]

    def leaving(device, chunk):
        return fields.at[:, :, pl.ds(pl.multiple_of(device * cells + chunk * LANES, LANES), LANES)]

    def copy(chunk, step):
        peer = lax.rem(me + step, n)
        return pltpu.make_async_remote_copy(
            src_ref=leaving(peer, chunk),
            dst_ref=landing(chunk),
            send_sem=send_sem.at[chunk, step],
            recv_sem=recv_sem.at[chunk, step],
            device_id={"cell": peer},
            device_id_type=MESH,
        )

    def own(chunk):
        return pltpu.make_async_copy(leaving(me, chunk), landing(chunk), own_sem.at[chunk])

    def out(chunk):
        at = pl.ds(pl.multiple_of(chunk * LANES, LANES), LANES)
        return pltpu.make_async_copy(ready.at[chunk], sens.at[:, at], out_sem.at[chunk])

    @pl.loop(0, chunks)
    def _(chunk):
        own(chunk).start()

        @pl.loop(1, n)
        def _(step):
            copy(chunk, step).start()

    squares[...] = jnp.zeros_like(squares)

    @pl.loop(0, chunks)
    def _(chunk):
        own(chunk).wait()

        @pl.loop(1, n)
        def _(step):
            copy(chunk, step).wait()

        chunk_sensitivities(
            quads, landed.at[chunk], coef.at[chunk], ready.at[chunk], squares, wide, diffs
        )
        out(chunk).start()

    @pl.loop(0, chunks)
    def _(chunk):
        out(chunk).wait()


def sensitivities(fields, quads, coef, n):
    comps, rows, _ = fields.shape
    chunks = coef.shape[0]
    electrodes, readings, cells = rows * n, quads.shape[0] // 4, chunks * LANES
    in_vmem = pl.BlockSpec(memory_space=pltpu.VMEM)
    anywhere = pl.BlockSpec(memory_space=pl.ANY)
    return pl.pallas_call(
        functools.partial(exchange_kernel, n),
        out_shape=[
            jax.ShapeDtypeStruct((readings * 4, cells), jnp.float32),
            jax.ShapeDtypeStruct((readings, LANES), jnp.float32),
        ],
        in_specs=[pl.BlockSpec(memory_space=pltpu.SMEM), anywhere, in_vmem],
        out_specs=[anywhere, in_vmem],
        scratch_shapes=[
            pltpu.VMEM((chunks, comps, electrodes, LANES), fields.dtype),
            pltpu.VMEM((chunks, readings * 4, LANES), jnp.float32),
            pltpu.VMEM((comps, electrodes, LANES), jnp.float32),
            pltpu.VMEM((2 * comps, readings, LANES), jnp.float32),
            pltpu.SemaphoreType.DMA((chunks, n)),
            pltpu.SemaphoreType.DMA((chunks, n)),
            pltpu.SemaphoreType.DMA((chunks,)),
            pltpu.SemaphoreType.DMA((chunks,)),
        ],
        compiler_params=pltpu.CompilerParams(
            collective_id=0, has_side_effects=True, vmem_limit_bytes=56 * 2**20
        ),
        name="exchange",
    )(quads, fields, coef)


def total_kernel(n, part, total, slots, send_sem, recv_sem):
    me = lax.axis_index("cell")
    greet(n, me)

    def copy(step):
        return pltpu.make_async_remote_copy(
            src_ref=part,
            dst_ref=slots.at[step],
            send_sem=send_sem.at[step],
            recv_sem=recv_sem.at[step],
            device_id={"cell": lax.rem(me + step, n)},
            device_id_type=MESH,
        )

    @pl.loop(1, n)
    def _(step):
        copy(step).start()

    slots[0] = part[...]

    @pl.loop(1, n)
    def _(step):
        copy(step).wait()

    total[...] = jnp.sum(slots[...], axis=0)


def total_of(part, n):
    return pl.pallas_call(
        functools.partial(total_kernel, n),
        out_shape=jax.ShapeDtypeStruct(part.shape, part.dtype),
        in_specs=[pl.BlockSpec(memory_space=pltpu.VMEM)],
        out_specs=pl.BlockSpec(memory_space=pltpu.VMEM),
        scratch_shapes=[
            pltpu.VMEM((n, *part.shape), part.dtype),
            pltpu.SemaphoreType.DMA((n,)),
            pltpu.SemaphoreType.DMA((n,)),
        ],
        compiler_params=pltpu.CompilerParams(collective_id=1, has_side_effects=True),
        name="total",
    )(part)


def norm_kernel(sens, scale, jacobian, coverage):
    count = sens.shape[0]

    @pl.when(pl.program_id(0) == 0)
    def _():
        coverage[...] = jnp.zeros_like(coverage)

    for lane in range(sens.shape[1] // LANES):
        at = pl.ds(lane * LANES, LANES)
        normed = sens[:, at] * scale[...]
        jacobian[:, :, at] = normed.reshape(count // 4, 4, LANES).astype(jnp.bfloat16)
        coverage[:, at] += jnp.sum((normed * normed).reshape(count // 8, 8, LANES), axis=0)


def normalise(sens, scale):
    rows, cells = sens.shape
    block = 1024
    return pl.pallas_call(
        norm_kernel,
        grid=(rows // block,),
        in_specs=[
            pl.BlockSpec((block, cells), lambda i: (i, 0)),
            pl.BlockSpec((block, LANES), lambda i: (i, 0)),
        ],
        out_specs=[
            pl.BlockSpec((block // 4, 4, cells), lambda i: (i, 0, 0)),
            pl.BlockSpec((8, cells), lambda i: (0, 0)),
        ],
        out_shape=[
            jax.ShapeDtypeStruct((rows // 4, 4, cells), jnp.bfloat16),
            jax.ShapeDtypeStruct((8, cells), jnp.float32),
        ],
        compiler_params=pltpu.CompilerParams(vmem_limit_bytes=48 * 2**20),
        name="norm",
    )(sens, scale)


def coefficients(horiz, vertical, tilt_angle, azimuth):
    sin_t, cos_t = jnp.sin(tilt_angle), jnp.cos(tilt_angle)
    sin_p, cos_p = jnp.sin(azimuth), jnp.cos(azimuth)
    axis = (sin_t * cos_p, sin_t * sin_p, cos_t)
    tilt = (cos_t * cos_p, cos_t * sin_p, -sin_t)
    turn = (-sin_t * sin_p, sin_t * cos_p, jnp.zeros_like(sin_t))
    contrast = vertical - horiz
    pairs = ((0, 0), (1, 1), (2, 2), (0, 1), (0, 2), (1, 2))
    rows = [-horiz * ((1.0 if i == j else 0.0) - axis[i] * axis[j]) for i, j in pairs]
    rows += [-vertical * axis[i] * axis[j] for i, j in pairs]
    for other in (tilt, turn):
        rows += [-contrast * (other[i] * axis[j] + axis[i] * other[j]) for i, j in pairs]
    return jnp.stack(rows)


def local(fields, horiz, vertical, tilt_angle, azimuth, electrode_quads):
    shards = lax.axis_size("cell")
    cells = horiz.shape[0]
    readings = electrode_quads.shape[0]
    coef = coefficients(horiz, vertical, tilt_angle, azimuth)
    coef = coef.reshape(coef.shape[0], cells // LANES, LANES).transpose(1, 0, 2)
    sens, squares = sensitivities(fields.transpose(1, 0, 2), electrode_quads.reshape(-1), coef, shards)
    part = jnp.sum(squares, axis=1).reshape(readings // LANES, LANES)
    meansq = total_of(part, shards).reshape(-1) / (4.0 * cells * shards)
    scale = jnp.broadcast_to(lax.rsqrt(meansq + 1e-06)[:, None, None], (readings, 4, LANES))
    jacobian, coverage = normalise(sens, scale.reshape(readings * 4, LANES))
    return jacobian, jnp.sum(coverage, axis=0)


def solution(mesh):
    placed = (
        P(("grp", "cell"), None, None),
        P(("grp", "cell")),
        P(("grp", "cell")),
        P(("grp", "cell")),
        P(("grp", "cell")),
        P("grp", None),
    )
    return jax.shard_map(
        local,
        mesh=mesh,
        in_specs=placed,
        out_specs=(P("grp", None, "cell"), P(("grp", "cell"))),
        check_vma=False,
    )
```

time: 396 us -> 334 us (0.84)
  Pallas kernels: 382 us -> 321 us
    pallas_call x1, Pallas kernels: 75.8 us -> 36.6 us  [total_of(): pl.pallas_call(functools.partial(total_kernel, n), out_shape=jax.ShapeDty...]
    pallas_call x2 -> x1, Pallas kernels: 295 us -> 272 us  [sensitivities(): pl.pallas_call(functools.partial(exchange_kernel, n), out_shape=[jax.Shap...]
where the time goes in v2:
time: 334 us
  Pallas kernels  321 us (96%)
  local copies, waits for them, and re-layouts  7.13 us (2%)
  other arithmetic  4.89 us (1%)
    pallas_call x1, Pallas kernels, sensitivities(): pl.pallas_call(functools.partial(exchange_kernel, n), out_shape=[jax.Shap...  272 us
    pallas_call x1, Pallas kernels, total_of(): pl.pallas_call(functools.partial(total_kernel, n), out_shape=jax.ShapeDty...  36.6 us
    pallas_call x1, Pallas kernels, normalise(): pl.pallas_call(norm_kernel, grid=(rows // block,), in_specs=[pl.BlockSpec...  12.2 us

profile of v2, /device:TPU:0, one launch (start us, length us, event | category | flops | bytes accessed | tf_op | source)
XLA Modules:
  0.0 333.9 jit_solution(444055698484116635)
XLA Ops:
  0.6 0.7 fusion.3
  1.4 0.7 add_multiply_fusion
  2.1 0.7 add_multiply_fusion.1
  2.8 1.9 stack.99
  4.7 1.1 copy.8
  5.8 1.2 reshape.74.quads
  7.1 272.4 %exchange.1 = (f32[8192,512]{1,0:T(8,128)}, f32[2048,128]{1,0:T(8,128)}) custom-call(s32[8192]{0:T(1024)} %reshape.74.quads, bf16[3,256,8192]{2,1,0:T(8,128)(2,1)} %bitcast.29, f32[4,24,128]{2,1,0:T(8,128)} %bitcast.30), custom_call_target="tpu_custom_call" | custom-call | tf_op jit(solution)/shard_map/exchange/pallas_call | solution.py:130
  279.5 2.2 reduce_sum.18
  281.6 36.6 %total.1 = f32[16,128]{1,0:T(8,128)} custom-call(f32[16,128]{1,0:T(8,128)} %bitcast.31), custom_call_target="tpu_custom_call" | custom-call | tf_op jit(solution)/shard_map/total/pallas_call | solution.py:183
  318.3 0.7 rsqrt_bitcast_fusion
  319.0 0.3 broadcast_in_dim.10
  319.3 0.6 broadcast_in_dim.11
  320.0 1.1 broadcast_in_dim.12.scale
  321.1 12.2 %norm.1 = (bf16[2048,4,512]{2,1,0:T(4,128)(2,1)}, f32[8,512]{1,0:T(8,128)S(1)}) custom-call(f32[8192,512]{1,0:T(8,128)} %get-tuple-element.6.sens, f32[8192,128]{1,0:T(8,128)S(1)} %broadcast_in_dim.12.scale), custom_call_target="tpu_custom_call" | custom-call | tf_op jit(solution)/shard_map/norm/pallas_call | solution.py:215
  333.3 0.6 reduce_sum.19

commit v3 on v2

--- a/solution.py
+++ b/solution.py
@@ -21,7 +21,21 @@
     pl.semaphore_wait(barrier, n - 1)
 
 
-def chunk_sensitivities(quads, grads, coef, sens, squares, wide, diffs):
+def fill_coefficients(coef, horiz, vertical, sin_t, cos_t, sin_p, cos_p):
+    axis = (sin_t * cos_p, sin_t * sin_p, cos_t)
+    tilt = (cos_t * cos_p, cos_t * sin_p, -sin_t)
+    turn = (-sin_t * sin_p, sin_t * cos_p, jnp.zeros_like(sin_t))
+    contrast = vertical - horiz
+    pairs = ((0, 0), (1, 1), (2, 2), (0, 1), (0, 2), (1, 2))
+    rows = [-horiz * ((1.0 if i == j else 0.0) - axis[i] * axis[j]) for i, j in pairs]
+    rows += [-vertical * axis[i] * axis[j] for i, j in pairs]
+    for other in (tilt, turn):
+        rows += [-contrast * (other[i] * axis[j] + axis[i] * other[j]) for i, j in pairs]
+    for k, row in enumerate(rows):
+        coef[k] = row
+
+
+def chunk_sensitivities(chunk, quads, grads, coef, sens, squares, wide, diffs):
     comps, electrodes, _ = wide.shape
     readings = squares.shape[0]
     block = 256
@@ -36,7 +50,7 @@
     def _(g):
         for u in range(8):
             q = g * 8 + u
-            a, b, m, n = (quads[4 * q + j] for j in range(4))
+            a, b, m, n = (quads[j, q] for j in range(4))
             for c in range(comps):
                 diffs[c, pl.ds(q, 1), :] = wide[c, pl.ds(a, 1), :] - wide[c, pl.ds(b, 1), :]
                 diffs[comps + c, pl.ds(q, 1), :] = wide[c, pl.ds(m, 1), :] - wide[c, pl.ds(n, 1), :]
@@ -52,16 +66,18 @@
         terms += [s[i] * r[j] + s[j] * r[i] for i, j in ((0, 1), (0, 2), (1, 2))]
         square = squares[pl.ds(at, tile), :]
         for p in range(4):
-            value = terms[0] * coef[pl.ds(6 * p, 1), :]
+            value = terms[0] * coef[6 * p, pl.ds(chunk, 1), :]
             for k in range(1, 6):
-                value = value + terms[k] * coef[pl.ds(6 * p + k, 1), :]
+                value = value + terms[k] * coef[6 * p + k, pl.ds(chunk, 1), :]
             sens[pl.ds(4 * at + p, tile, stride=4), :] = value
             square = square + value * value
         squares[pl.ds(at, tile), :] = square
 
 
 def exchange_kernel(
-    n, quads, fields, coef, sens, squares, landed, ready, wide, diffs, send_sem, recv_sem, own_sem, out_sem
+    n, quads, fields, horiz, vertical, sin_t, cos_t, sin_p, cos_p, sens, total,
+    landed, ready, wide, diffs, squares, coef, part, slots,
+    send_sem, recv_sem, own_sem, out_sem, part_send_sem, part_recv_sem,
 ):
     me = lax.axis_index("cell")
     rows = fields.shape[1]
@@ -102,6 +118,7 @@
             copy(chunk, step).start()
 
     squares[...] = jnp.zeros_like(squares)
+    fill_coefficients(coef, *(x[...] for x in (horiz, vertical, sin_t, cos_t, sin_p, cos_p)))
 
     @pl.loop(0, chunks)
     def _(chunk):
@@ -112,87 +129,75 @@
             copy(chunk, step).wait()
 
         chunk_sensitivities(
-            quads, landed.at[chunk], coef.at[chunk], ready.at[chunk], squares, wide, diffs
+            chunk, quads, landed.at[chunk], coef, ready.at[chunk], squares, wide, diffs
         )
         out(chunk).start()
+
+    def copy_part(step):
+        return pltpu.make_async_remote_copy(
+            src_ref=part,
+            dst_ref=slots.at[step],
+            send_sem=part_send_sem.at[step],
+            recv_sem=part_recv_sem.at[step],
+            device_id={"cell": lax.rem(me + step, n)},
+            device_id_type=MESH,
+        )
+
+    part[...] = jnp.sum(squares[...].reshape(*part.shape, LANES), axis=-1)
+
+    @pl.loop(1, n)
+    def _(step):
+        copy_part(step).start()
+
+    slots[0] = part[...]
 
     @pl.loop(0, chunks)
     def _(chunk):
         out(chunk).wait()
 
-
-def sensitivities(fields, quads, coef, n):
+    @pl.loop(1, n)
+    def _(step):
+        copy_part(step).wait()
+
+    total[...] = jnp.sum(slots[...], axis=0)
+
+
+def sensitivities(fields, quads, cell_values, n):
     comps, rows, _ = fields.shape
-    chunks = coef.shape[0]
-    electrodes, readings, cells = rows * n, quads.shape[0] // 4, chunks * LANES
+    chunks = cell_values[0].shape[0]
+    electrodes, readings, cells = rows * n, quads.shape[1], chunks * LANES
+    sums = (readings // LANES, LANES)
     in_vmem = pl.BlockSpec(memory_space=pltpu.VMEM)
     anywhere = pl.BlockSpec(memory_space=pl.ANY)
     return pl.pallas_call(
         functools.partial(exchange_kernel, n),
         out_shape=[
             jax.ShapeDtypeStruct((readings * 4, cells), jnp.float32),
-            jax.ShapeDtypeStruct((readings, LANES), jnp.float32),
-        ],
-        in_specs=[pl.BlockSpec(memory_space=pltpu.SMEM), anywhere, in_vmem],
+            jax.ShapeDtypeStruct(sums, jnp.float32),
+        ],
+        in_specs=[pl.BlockSpec(memory_space=pltpu.SMEM), anywhere] + [in_vmem] * len(cell_values),
         out_specs=[anywhere, in_vmem],
         scratch_shapes=[
             pltpu.VMEM((chunks, comps, electrodes, LANES), fields.dtype),
             pltpu.VMEM((chunks, readings * 4, LANES), jnp.float32),
             pltpu.VMEM((comps, electrodes, LANES), jnp.float32),
             pltpu.VMEM((2 * comps, readings, LANES), jnp.float32),
+            pltpu.VMEM((readings, LANES), jnp.float32),
+            pltpu.VMEM((24, chunks, LANES), jnp.float32),
+            pltpu.VMEM(sums, jnp.float32),
+            pltpu.VMEM((n, *sums), jnp.float32),
             pltpu.SemaphoreType.DMA((chunks, n)),
             pltpu.SemaphoreType.DMA((chunks, n)),
             pltpu.SemaphoreType.DMA((chunks,)),
             pltpu.SemaphoreType.DMA((chunks,)),
+            pltpu.SemaphoreType.DMA((n,)),
+            pltpu.SemaphoreType.DMA((n,)),
         ],
         compiler_params=pltpu.CompilerParams(
             collective_id=0, has_side_effects=True, vmem_limit_bytes=56 * 2**20
         ),
         name="exchange",
-    )(quads, fields, coef)
-
-
-def total_kernel(n, part, total, slots, send_sem, recv_sem):
-    me = lax.axis_index("cell")
-    greet(n, me)
-
-    def copy(step):
-        return pltpu.make_async_remote_copy(
-            src_ref=part,
-            dst_ref=slots.at[step],
-            send_sem=send_sem.at[step],
-            recv_sem=recv_sem.at[step],
-            device_id={"cell": lax.rem(me + step, n)},
-            device_id_type=MESH,
-        )
-
-    @pl.loop(1, n)
-    def _(step):
-        copy(step).start()
-
-    slots[0] = part[...]
-
-    @pl.loop(1, n)
-    def _(step):
-        copy(step).wait()
-
-    total[...] = jnp.sum(slots[...], axis=0)
-
-
-def total_of(part, n):
-    return pl.pallas_call(
-        functools.partial(total_kernel, n),
-        out_shape=jax.ShapeDtypeStruct(part.shape, part.dtype),
-        in_specs=[pl.BlockSpec(memory_space=pltpu.VMEM)],
-        out_specs=pl.BlockSpec(memory_space=pltpu.VMEM),
-        scratch_shapes=[
-            pltpu.VMEM((n, *part.shape), part.dtype),
-            pltpu.SemaphoreType.DMA((n,)),
-            pltpu.SemaphoreType.DMA((n,)),
-        ],
-        compiler_params=pltpu.CompilerParams(collective_id=1, has_side_effects=True),
-        name="total",
-    )(part)
+    )(quads, fields, *cell_values)
 
 
 def norm_kernel(sens, scale, jacobian, coverage):
@@ -232,30 +237,20 @@
     )(sens, scale)
 
 
-def coefficients(horiz, vertical, tilt_angle, azimuth):
-    sin_t, cos_t = jnp.sin(tilt_angle), jnp.cos(tilt_angle)
-    sin_p, cos_p = jnp.sin(azimuth), jnp.cos(azimuth)
-    axis = (sin_t * cos_p, sin_t * sin_p, cos_t)
-    tilt = (cos_t * cos_p, cos_t * sin_p, -sin_t)
-    turn = (-sin_t * sin_p, sin_t * cos_p, jnp.zeros_like(sin_t))
-    contrast = vertical - horiz
-    pairs = ((0, 0), (1, 1), (2, 2), (0, 1), (0, 2), (1, 2))
-    rows = [-horiz * ((1.0 if i == j else 0.0) - axis[i] * axis[j]) for i, j in pairs]
-    rows += [-vertical * axis[i] * axis[j] for i, j in pairs]
-    for other in (tilt, turn):
-        rows += [-contrast * (other[i] * axis[j] + axis[i] * other[j]) for i, j in pairs]
-    return jnp.stack(rows)
-
-
 def local(fields, horiz, vertical, tilt_angle, azimuth, electrode_quads):
     shards = lax.axis_size("cell")
     cells = horiz.shape[0]
     readings = electrode_quads.shape[0]
-    coef = coefficients(horiz, vertical, tilt_angle, azimuth)
-    coef = coef.reshape(coef.shape[0], cells // LANES, LANES).transpose(1, 0, 2)
-    sens, squares = sensitivities(fields.transpose(1, 0, 2), electrode_quads.reshape(-1), coef, shards)
-    part = jnp.sum(squares, axis=1).reshape(readings // LANES, LANES)
-    meansq = total_of(part, shards).reshape(-1) / (4.0 * cells * shards)
+    values = (
+        horiz, vertical, jnp.sin(tilt_angle), jnp.cos(tilt_angle), jnp.sin(azimuth), jnp.cos(azimuth)
+    )
+    sens, total = sensitivities(
+        fields.transpose(1, 0, 2),
+        electrode_quads.T,
+        [x.reshape(cells // LANES, LANES) for x in values],
+        shards,
+    )
+    meansq = total.reshape(-1) / (4.0 * cells * shards)
     scale = jnp.broadcast_to(lax.rsqrt(meansq + 1e-06)[:, None, None], (readings, 4, LANES))
     jacobian, coverage = normalise(sens, scale.reshape(readings * 4, LANES))
     return jacobian, jnp.sum(coverage, axis=0)

time: 334 us -> 324 us (0.970)
  local copies, waits for them, and re-layouts: 7.13 us -> 3.45 us
  other arithmetic: 4.89 us -> 1.3 us
    pallas_call x1 -> x0, Pallas kernels: 36.6 us -> none  [total_of(): pl.pallas_call(functools.partial(total_kernel, n), out_shape=jax.ShapeDty...]
    pallas_call x1, Pallas kernels: 272 us -> 306 us  [sensitivities(): pl.pallas_call(functools.partial(exchange_kernel, n), out_shape=[jax.Shap...]
where the time goes in v3:
time: 324 us; the launch traced here: 323 us
  Pallas kernels  318 us (98%)
  local copies, waits for them, and re-layouts  3.45 us (1%)
    pallas_call x1, Pallas kernels, sensitivities(): pl.pallas_call(functools.partial(exchange_kernel, n), out_shape=[jax.Shap...  306 us
    pallas_call x1, Pallas kernels, normalise(): pl.pallas_call(norm_kernel, grid=(rows // block,), in_specs=[pl.BlockSpec...  12.2 us

profile of v3, /device:TPU:0, one launch (start us, length us, event | category | flops | bytes accessed | tf_op | source)
XLA Modules:
  0.0 323.3 jit_solution(16970999901696387120)
XLA Ops:
  0.6 1.3 cosine_bitcast_fusion
  2.0 305.8 %exchange.1 = (f32[8192,512]{1,0:T(8,128)}, f32[16,128]{1,0:T(8,128)}) custom-call(s32[4,2048]{1,0:T(4,128)} %bitcast.15, bf16[3,256,8192]{2,1,0:T(8,128)(2,1)} %bitcast.14, f32[4,128]{1,0:T(4,128)} %bitcast.16, f32[4,128]{1,0:T(4,128)} %bitcast.17, f32[4,128]{1,0:T(4,128)} %get-tuple-element.14.sin_t, f32[4,128]{1,0:T(4,128)} %get-tuple-element.15.cos_t, ...), custom_call_target="tpu_custom_call" | custom-call | tf_op jit(solution)/shard_map/exchange/pallas_call | solution.py:172
  307.8 0.7 rsqrt_bitcast_fusion
  308.5 0.3 broadcast_in_dim.10
  308.8 0.6 broadcast_in_dim.11
  309.4 1.1 broadcast_in_dim.12.scale
  310.6 12.2 %norm.1 = (bf16[2048,4,512]{2,1,0:T(4,128)(2,1)}, f32[8,512]{1,0:T(8,128)S(1)}) custom-call(f32[8192,512]{1,0:T(8,128)} %get-tuple-element.6.sens, f32[8192,128]{1,0:T(8,128)S(1)} %broadcast_in_dim.12.scale), custom_call_target="tpu_custom_call" | custom-call | tf_op jit(solution)/shard_map/norm/pallas_call | solution.py:220
  322.8 0.6 reduce_sum.9

commit v4 on v3

--- a/solution.py
+++ b/solution.py
@@ -48,12 +48,15 @@
 
     @pl.loop(0, readings // 8)
     def _(g):
+        at = pl.multiple_of(g * 8, 8)
+        rows = []
         for u in range(8):
-            q = g * 8 + u
-            a, b, m, n = (quads[j, q] for j in range(4))
-            for c in range(comps):
-                diffs[c, pl.ds(q, 1), :] = wide[c, pl.ds(a, 1), :] - wide[c, pl.ds(b, 1), :]
-                diffs[comps + c, pl.ds(q, 1), :] = wide[c, pl.ds(m, 1), :] - wide[c, pl.ds(n, 1), :]
+            a, b, m, n = (quads[j, at + u] for j in range(4))
+            rows += [wide[c, pl.ds(a, 1), :] - wide[c, pl.ds(b, 1), :] for c in range(comps)]
+            rows += [wide[c, pl.ds(m, 1), :] - wide[c, pl.ds(n, 1), :] for c in range(comps)]
+        for u in range(8):
+            for c in range(2 * comps):
+                diffs[c, pl.ds(at + u, 1), :] = rows[2 * comps * u + c]
 
     tile = 16
 

time: 324 us -> 324 us (level)
  no operation moved by 1% of the time
where the time goes in v4:
time: 324 us; the launch traced here: 323 us
  Pallas kernels  318 us (98%)
  local copies, waits for them, and re-layouts  3.45 us (1%)
    pallas_call x1, Pallas kernels, sensitivities(): pl.pallas_call(functools.partial(exchange_kernel, n), out_shape=[jax.Shap...  306 us
    pallas_call x1, Pallas kernels, normalise(): pl.pallas_call(norm_kernel, grid=(rows // block,), in_specs=[pl.BlockSpec...  12.2 us

profile of v4, /device:TPU:0, one launch (start us, length us, event | category | flops | bytes accessed | tf_op | source)
XLA Modules:
  0.0 323.3 jit_solution(2146307126289838958)
XLA Ops:
  0.6 1.3 cosine_bitcast_fusion
  2.0 305.8 %exchange.1 = (f32[8192,512]{1,0:T(8,128)}, f32[16,128]{1,0:T(8,128)}) custom-call(s32[4,2048]{1,0:T(4,128)} %bitcast.15, bf16[3,256,8192]{2,1,0:T(8,128)(2,1)} %bitcast.14, f32[4,128]{1,0:T(4,128)} %bitcast.16, f32[4,128]{1,0:T(4,128)} %bitcast.17, f32[4,128]{1,0:T(4,128)} %get-tuple-element.14.sin_t, f32[4,128]{1,0:T(4,128)} %get-tuple-element.15.cos_t, ...), custom_call_target="tpu_custom_call" | custom-call | tf_op jit(solution)/shard_map/exchange/pallas_call | solution.py:175
  307.8 0.7 rsqrt_bitcast_fusion
  308.5 0.3 broadcast_in_dim.10
  308.8 0.6 broadcast_in_dim.11
  309.4 1.1 broadcast_in_dim.12.scale
  310.6 12.2 %norm.1 = (bf16[2048,4,512]{2,1,0:T(4,128)(2,1)}, f32[8,512]{1,0:T(8,128)S(1)}) custom-call(f32[8192,512]{1,0:T(8,128)} %get-tuple-element.6.sens, f32[8192,128]{1,0:T(8,128)S(1)} %broadcast_in_dim.12.scale), custom_call_target="tpu_custom_call" | custom-call | tf_op jit(solution)/shard_map/norm/pallas_call | solution.py:223
  322.8 0.6 reduce_sum.9
